TPU v7x, 32 devices: a whole 2x2x4 slice. The times are simulated.
32 devices in a mesh: grp: 4 (over y, core), tp: 2 (over x), seq: 4 (over z).
Axes of the slice: x: 2, y: 2, z: 4, core: 2. Of those that a mesh axis runs over, the one named last changes fastest.
Arguments:
- crops: bfloat16 [4, 4, 576, 1024], P('grp', 'seq', 'tp'), may hold values from -6 to 6
- dout: bfloat16 [4, 4, 576, 1024], P('grp', 'seq', None, 'tp'), may hold values from -0.796875 to 0.796875
- crop_count: int32 [4], P('grp'), may hold values from 2 to 4, as said below
- crop_ids: int32 [4, 4], P('grp'), may hold values from 0 to 3, each once within a row
- seq_slot: int32 [4, 4], P('grp'), may hold values from 0 to 3, as said below
- norm_gain: bfloat16 [1024], replicated, may hold values from 0.099609375 to 1.8984375
- qkv_weight: bfloat16 [3, 1024, 1024], P(None, None, 'tp'), may hold values from -40 to 40
Outputs:
- weight_grad: float32 [3072, 1024], P(('grp', 'seq'), 'tp')
Inputs may be any that keep to these rules, and one draw needn't show every extreme that they name: `crop_count`: some page selects 4 crops. `seq_slot`: distinct within a row; only the first crop_count entries of a row are used. `crop_ids`: only the first crop_count entries of a row are used.
All inputs are finite; a program needn't handle non-finite values.
Results may differ from a plain program's by a relative error of at most 0.0084.
Values may be sent and summed in bfloat16 or wider, within the bound.
A program may use at most 64 MiB of HBM per device.

v0:
```python
import jax
import jax.numpy as jnp
from jax import lax
from jax.sharding import PartitionSpec as P

HD = 64


def crop_grads(inputs, cotangent, norm_gain, weight):
    crops_here, tok_count, head_cols = cotangent.shape
    head_count = head_cols // HD
    values = inputs.astype(jnp.float32)
    centred = values - jnp.mean(values, axis=-1, keepdims=True)
    spread = jnp.mean(centred * centred, axis=-1, keepdims=True)
    normed = (centred * lax.rsqrt(spread + 1e-05) * norm_gain.astype(jnp.float32)).astype(
        jnp.bfloat16
    )
    projected = jnp.einsum(
        "etd,cdw->cetw", normed, weight, preferred_element_type=jnp.float32
    ).astype(jnp.bfloat16)
    heads_view = projected.reshape(3, crops_here, tok_count, head_count, HD)
    queries = heads_view[0]
    key_rows = heads_view[1]
    value_rows = heads_view[2]
    score_scale = HD ** (-0.5)
    scores = (
        jnp.einsum("eqhd,ekhd->ehqk", queries, key_rows, preferred_element_type=jnp.float32)
        * score_scale
    )
    attention = jax.nn.softmax(scores, axis=-1)
    attention_low = attention.astype(jnp.bfloat16)
    upstream = cotangent.reshape(crops_here, tok_count, head_count, HD)
    grad_values = jnp.einsum(
        "ehqk,eqhd->ekhd", attention_low, upstream, preferred_element_type=jnp.float32
    ).astype(jnp.bfloat16)
    grad_attention = jnp.einsum(
        "eqhd,ekhd->ehqk", upstream, value_rows, preferred_element_type=jnp.float32
    )
    grad_scores = attention * (
        grad_attention - jnp.sum(attention * grad_attention, axis=-1, keepdims=True)
    )
    scaled = (grad_scores * score_scale).astype(jnp.bfloat16)
    grad_queries = jnp.einsum(
        "ehqk,ekhd->eqhd", scaled, key_rows, preferred_element_type=jnp.float32
    ).astype(jnp.bfloat16)
    grad_keys = jnp.einsum(
        "ehqk,eqhd->ekhd", scaled, queries, preferred_element_type=jnp.float32
    ).astype(jnp.bfloat16)
    stacked = jnp.stack([grad_queries, grad_keys, grad_values]).reshape(
        3, crops_here, tok_count, head_cols
    )
    return jnp.einsum("etd,cetw->cdw", normed, stacked, preferred_element_type=jnp.float32)


def body(crops, dout, crop_count, crop_ids, seq_slot, norm_gain, qkv_weight):
    seq_index = lax.axis_index("seq")
    model_width = crops.shape[3]
    slot_local = dout.shape[1]
    head_cols = dout.shape[3]
    most_crops = crop_ids.shape[1]
    rank_range = jnp.arange(most_crops, dtype=jnp.int32)
    is_live = (rank_range < crop_count[0]).astype(jnp.float32)
    choose_crop = (crop_ids[0][:, None] == rank_range[None, :]).astype(jnp.float32) * is_live[
        :, None
    ]
    wanted = seq_index * slot_local + jnp.arange(slot_local, dtype=jnp.int32)
    slot_rows = (seq_slot[0][None, :] == wanted[:, None]).astype(jnp.float32)
    selector = jnp.dot(slot_rows, choose_crop).astype(jnp.bfloat16)
    gathered = jnp.einsum(
        "sc,ctd->std",
        selector,
        lax.all_gather(crops, "seq", axis=1, tiled=True)[0],
        preferred_element_type=jnp.float32,
    )
    cotangent = dout[0]
    local_tokens = gathered.astype(jnp.bfloat16)
    full_crops = lax.all_gather(local_tokens, "tp", axis=1, tiled=True)
    local_grad = crop_grads(full_crops, cotangent, norm_gain, qkv_weight)
    grad_rows = local_grad.reshape(3 * model_width, head_cols)
    return lax.psum_scatter(grad_rows, ("grp", "seq"), scatter_dimension=0, tiled=True)


def solution(mesh):
    in_specs = (
        P("grp", "seq", "tp", None),
        P("grp", "seq", None, "tp"),
        P("grp"),
        P("grp", None),
        P("grp", None),
        P(),
        P(None, None, "tp"),
    )
    out_specs = P(("grp", "seq"), "tp")
    return jax.shard_map(body, mesh=mesh, in_specs=in_specs, out_specs=out_specs, check_vma=False)
```

profile of v0, /device:TPU:0, one launch (start us, length us, event | category | flops | bytes accessed | tf_op | source)
XLA Modules:
  0.0 279.6 jit_solution(7304586487090792497)
XLA Ops:
  6.5 0.7 all-gather.4.cloned.1.call-update
  8.1 54.0 %all-gather.4.cloned.1.call-done = bf16[1,4,288,1024]{3,2,0,1:T(8,128)(2,1)} async-done(((bf16[1,1,288,1024]{3,2,0,1:T(8,128)(2,1)}), bf16[1,4,288,1024]{3,2,0,1:T(8,128)(2,1)}) %all-gather.4.cloned.1.call-update) | async-done | bytes 2359312 | tf_op jit(solution)/shard_map/all_gather | solution.py:72
  62.1 4.8 %fusion.20 = bf16[1,288,1024]{2,0,1:T(2,128)(2,1)} fusion(bf16[4,288,1024]{2,1,0:T(8,128)(2,1)} %bitcast.134, s32[1,4]{1,0:T(1,128)} %param.11, bf16[4]{0:T(256)(128)(2,1)S(1)} %compare_convert_fusion, s32[4]{0:T(128)} %bitcast.135, s32[]{:T(128)S(6)} %axis_index.12), kind=kOutput, calls=%fused_computation.26 | convolution fusion | flops 2359364 | bytes 2949164 | tf_op jit(solution)/shard_map/sc,ctd->std/dot_general | solution.py:69
  66.9 2.3 copy.52
  69.5 2.2 copy.36
  71.7 19.3 %all-gather.6.cloned.1.call-done = bf16[576,1024]{1,0:T(8,128)(2,1)} async-done(((bf16[288,1024]{1,0:T(8,128)(2,1)}), bf16[576,1024]{1,0:T(8,128)(2,1)}) %all-gather.6.cloned.1.call-update) | async-done | bytes 1179664 | tf_op jit(solution)/shard_map/all_gather | solution.py:77
  91.0 1.5 convert_reduce_fusion
  92.5 1.7 fusion.17
  94.2 3.4 %convert_bitcast_fusion.1 = bf16[3,1,576,512]{3,2,0,1:T(8,128)(2,1)S(1)} fusion(bf16[3,1024,512]{2,1,0:T(8,128)(2,1)S(1)} %copy-done, bf16[576,1024]{1,0:T(8,128)(2,1)} %all-gather.6.cloned.1.call-done, f32[1024]{0:T(1024)S(1)} %convert_element_type.83, f32[576]{0:T(1024)S(1)} %add_rsqrt_fusion, f32[576]{0:T(1024)S(1)} %broadcast_multiply_fusion), kind=kOutput, calls=%fused_computation.33 | convolution fusion | flops 1815773184 | bytes 6103552 | tf_op jit(solution)/shard_map/etd,cdw->cetw/dot_general | solution.py:18
  97.6 1.3 fusion.60
  99.0 2.1 copy.35
  101.1 2.2 copy.34
  103.3 2.1 copy.33
  105.4 7.4 %fusion.62 = f32[8,576,576]{2,1,0:T(8,128)} fusion(bf16[576,8,64]{0,2,1:T(8,128)(2,1)} %bitcast.124, bf16[576,8,64]{0,2,1:T(8,128)(2,1)} %bitcast.122), kind=kOutput, calls=%fused_computation.63 | convolution fusion | flops 339738624 | bytes 11796480 | tf_op jit(solution)/shard_map/eqhd,ekhd->ehqk/dot_general | solution.py:36
  112.9 9.2 %fusion.61 = (f32[8,576]{1,0:T(8,128)S(1)}, f32[8,576,576]{1,2,0:T(8,128)}) fusion(bf16[576,8,64]{0,2,1:T(8,128)(2,1)} %bitcast.126, bf16[576,8,64]{0,2,1:T(8,128)(2,1)} %bitcast.128), kind=kOutput, calls=%fused_computation.62 | convolution fusion | flops 347701824 | bytes 11814912 | tf_op jit(solution)/shard_map/sub | solution.py:30
  122.1 7.1 %fusion.28 = bf16[8,576,64]{1,2,0:T(8,128)(2,1)} fusion(bf16[576,8,64]{0,2,1:T(8,128)(2,1)} %bitcast.123, f32[8,576,576]{1,2,0:T(8,128)} %get-tuple-element.9, f32[8,576]{1,0:T(8,128)S(1)} %get-tuple-element.8), kind=kOutput, calls=%fused_computation.35 | convolution fusion | flops 345341952 | bytes 11814912 | tf_op jit(solution)/shard_map/ehqk,eqhd->ekhd/dot_general | solution.py:33
  129.2 19.0 %fusion.32 = bf16[8,64,576]{2,1,0:T(8,128)(2,1)} fusion(bf16[576,8,64]{0,2,1:T(8,128)(2,1)} %bitcast.127, f32[8,576,576]{2,1,0:T(8,128)} %fusion.62, f32[8,576,576]{1,2,0:T(8,128)} %get-tuple-element.9, f32[8,576]{1,0:T(8,128)S(1)} %get-tuple-element.8), kind=kOutput, calls=%fused_computation.37 | convolution fusion | flops 358618176 | bytes 22431744 | tf_op jit(solution)/shard_map/ehqk,eqhd->ekhd/dot_general | solution.py:46
  148.2 19.1 %fusion.31 = bf16[8,64,576]{2,1,0:T(8,128)(2,1)} fusion(bf16[576,8,64]{0,2,1:T(8,128)(2,1)} %bitcast.129, f32[8,576,576]{2,1,0:T(8,128)} %fusion.62, f32[8,576,576]{1,2,0:T(8,128)} %get-tuple-element.9, f32[8,576]{1,0:T(8,128)S(1)} %get-tuple-element.8), kind=kOutput, calls=%fused_computation.36 | convolution fusion | flops 358618176 | bytes 22431744 | tf_op jit(solution)/shard_map/ehqk,ekhd->eqhd/dot_general | solution.py:43
  167.3 2.1 copy.42
  169.5 2.1 copy.40
  171.6 2.2 copy.41
  173.8 7.3 %convolution_bitcast_fusion = f32[3,1024,512]{1,2,0:T(8,128)} fusion(bf16[1,1,576,512]{3,2,0,1:T(8,128)(2,1)} %copy.42, bf16[1,1,576,512]{3,2,0,1:T(8,128)(2,1)} %copy.41, bf16[1,1,576,512]{3,2,0,1:T(8,128)(2,1)} %copy.40, bf16[576,1024]{1,0:T(8,128)(2,1)} %all-gather.6.cloned.1.call-done, f32[1024]{0:T(1024)S(1)} %convert_element_type.83, ...), kind=kOutput, calls=%fused_computation.19 | convolution fusion | flops 1816657920 | bytes 9249280 | tf_op jit(solution)/shard_map/etd,cetw->cdw/dot_general | solution.py:52
  181.1 6.6 %copy.43 = f32[3,1024,512]{2,1,0:T(8,128)} copy(f32[3,1024,512]{1,2,0:T(8,128)} %convolution_bitcast_fusion) | data formatting | bytes 12582912 | tf_op jit(solution)/shard_map/etd,cetw->cdw/transpose | solution.py:52
  187.7 85.4 %reduce-scatter.2.cloned.1.call-done = f32[192,512]{1,0:T(8,128)} async-done(((f32[3072,512]{1,0:T(8,128)}), f32[192,512]{1,0:T(8,128)}) %reduce-scatter.2.cloned.1.call-update) | async-done | bytes 393232 | tf_op jit(solution)/shard_map/reduce_scatter | solution.py:80
  (13 shorter events, 0.3 us)
Async XLA Ops:
  6.5 87.7 %copy-start = (bf16[3,1024,512]{2,1,0:T(8,128)(2,1)S(1)}, bf16[3,1024,512]{2,1,0:T(8,128)(2,1)}, u32[]{:S(2)}) copy-start(bf16[3,1024,512]{2,1,0:T(8,128)(2,1)} %param.13) | copy-start | bytes 9437188
  6.5 62.9 %copy-start.1 = (bf16[1024]{0:T(1024)(128)(2,1)S(1)}, bf16[1024]{0:T(1024)(128)(2,1)}, u32[]{:S(2)}) copy-start(bf16[1024]{0:T(1024)(128)(2,1)} %param.12) | copy-start | bytes 6148
  6.5 55.6 %all-gather.4.cloned.1.call-start = ((), (), s32[]{:S(2)}) async-start(), calls=%async_computation.1 | async-start | bytes 2949120 | tf_op jit(solution)/shard_map/all_gather | solution.py:72
  7.3 83.7 %all-gather.6.cloned.1.call-start = ((), (), s32[]{:S(2)}) async-start(), calls=%async_computation.3 | async-start | bytes 1769472 | tf_op jit(solution)/shard_map/all_gather | solution.py:77
  69.2 203.9 %reduce-scatter.2.cloned.1.call-start = ((), (), s32[]{:S(2)}) async-start(), calls=%async_computation.2 | async-start | bytes 6684672 | tf_op jit(solution)/shard_map/reduce_scatter | solution.py:80
Sparse Core Ops, SparseCore 0:
  8.9 53.1 all-gather.3
  69.4 21.5 all-gather.5
  187.8 85.2 reduce-scatter.1
where the time goes:
time: 280 us
  waiting for transfers between devices  159 us (57%)
  matrix products  77.4 us (28%)
  local copies, waits for them, and re-layouts  25.3 us (9%)
  between operations  14 us (5%)
  other arithmetic  3.26 us (1%)
    reduce_scatter x1, waiting for transfers between devices, body(): lax.psum_scatter(grad_rows, ('grp', 'seq'), scatter_dimension=0, tiled=True)  85.4 us
    all_gather x1, waiting for transfers between devices, body(): lax.all_gather(crops, 'seq', axis=1, tiled=True)[0]  54 us
    all_gather x1, waiting for transfers between devices, body(): full_crops = lax.all_gather(local_tokens, 'tp', axis=1, tiled=True)  19.3 us
    dot_general x1, matrix products, crop_grads(): jnp.einsum('ehqk,ekhd->eqhd', scaled, key_rows, preferred_element_type=jn...  19.1 us
    dot_general x1, matrix products, crop_grads(): jnp.einsum('ehqk,eqhd->ekhd', scaled, queries, preferred_element_type=jnp...  19 us
    sub x1, matrix products, crop_grads(): attention = jax.nn.softmax(scores, axis=-1)  9.23 us
    dot_general x1, matrix products, crop_grads(): jnp.einsum('eqhd,ekhd->ehqk', upstream, value_rows, preferred_element_typ...  7.42 us
    dot_general x1, matrix products, crop_grads(): jnp.einsum('etd,cetw->cdw', normed, stacked, preferred_element_type=jnp.f...  7.31 us
  transfers between devices with their start and end apart: 3, of which 3 were waited for; matrix products, arithmetic and copies ran while one was open for 1% of the time, Pallas kernels for 0%

commit v1 on v0

v1 whole, which is shorter than its diff:
```python
import functools

import jax
import jax.numpy as jnp
from jax import lax
from jax.experimental import pallas as pl
from jax.experimental.pallas import tpu as pltpu
from jax.sharding import PartitionSpec as P

HD = 64
LANES = 128
MESH = pl.DeviceIdType.MESH
LOG2E = 1.4426950408889634
F32 = jnp.float32
BF16 = jnp.bfloat16


def mm(a, b, ca, cb):
    return lax.dot_general(a, b, (((ca,), (cb,)), ((), ())), preferred_element_type=F32)


def kernel(
    sizes,
    x_ref,
    g_ref,
    count_ref,
    ids_ref,
    slot_ref,
    gain_ref,
    w_hbm,
    out_ref,
    w_ref,
    x_all,
    normed32,
    normed,
    normed_t,
    proj,
    g_all,
    total,
    acc,
    s1,
    r1,
    s2,
    r2,
    s3,
    r3,
    w_sem,
    xs_sem,
    xr_sem,
    gs_sem,
    gr_sem,
    s1_sem,
    r1_sem,
    s2_sem,
    r2_sem,
    s3_sem,
    r3_sem,
):
    n_grp, n_tp, n_seq, n_core = sizes
    n_y = n_grp // n_core
    grp = lax.axis_index("grp")
    tp = lax.axis_index("tp")
    seq = lax.axis_index("seq")
    y = grp // n_core
    core = grp % n_core
    other = n_core - 1 - core
    groups = proj.shape[1]
    tokens = proj.shape[2]
    width = w_ref.shape[1]
    pieces, piece_rows = x_all.shape[1], x_all.shape[2]
    out_rows = out_ref.shape[0]
    block_rows = n_seq * out_rows
    hops = n_seq - 1

    def at(g=None, t=None, s=None):
        return (grp if g is None else g, tp if t is None else t, seq if s is None else s)

    partners = [at(t=(tp + d) % n_tp) for d in range(1, n_tp)]
    partners += [at(s=(seq + d) % n_seq) for d in range(1, n_seq)]
    partners += [at(g=((y + d) % n_y) * n_core + core) for d in range(1, n_y)]
    if n_core > 1:
        partners += [at(g=y * n_core + other)]

    w_copy = pltpu.make_async_copy(w_hbm, w_ref, w_sem)
    w_copy.start()
    barrier = pltpu.get_barrier_semaphore()
    for partner in partners:
        pl.semaphore_signal(barrier, inc=1, device_id=partner, device_id_type=MESH)
    pl.semaphore_wait(barrier, len(partners))

    def x_copy(d, piece):
        return pltpu.make_async_remote_copy(
            src_ref=x_ref.at[piece],
            dst_ref=x_all.at[d, piece],
            send_sem=xs_sem.at[d - 1, piece],
            recv_sem=xr_sem.at[d - 1, piece],
            device_id=at(t=(tp + n_tp - d) % n_tp),
            device_id_type=MESH,
        )

    for piece in range(pieces):
        for d in range(1, n_tp):
            x_copy(d, piece).start()

    def g_copy(way, hop, group):
        step = 1 if way == 0 else -1
        block = seq - step * hop
        return pltpu.make_async_remote_copy(
            src_ref=g_all.at[block, group],
            dst_ref=g_all.at[block, group],
            send_sem=gs_sem.at[way, hop, group],
            recv_sem=gr_sem.at[way, hop, group],
            device_id=at(s=seq + step),
            device_id_type=MESH,
        )

    def g_wait_copy(way, hop, group):
        step = 1 if way == 0 else -1
        block = seq - step * (hop + 1)
        return pltpu.make_async_remote_copy(
            src_ref=g_all.at[block, group],
            dst_ref=g_all.at[block, group],
            send_sem=gs_sem.at[way, hop, group],
            recv_sem=gr_sem.at[way, hop, group],
            device_id=at(s=seq - step),
            device_id_type=MESH,
        )

    def sends(way, hop):
        if way == 0:
            return (seq >= hop) & (seq + 1 < n_seq)
        return (seq + hop < n_seq) & (seq >= 1)

    def receives(way, hop):
        return seq >= hop + 1 if way == 0 else seq + hop + 1 < n_seq

    def g_level(level):
        for way in range(2):

            @pl.when((level < groups) & sends(way, 0))
            def _():
                g_copy(way, 0, level).start()

        for hop in range(hops - 1, -1, -1):
            group = level - 1 - hop
            inside = (group >= 0) & (group < groups)
            for way in range(2):

                @pl.when(inside & receives(way, hop))
                def _():
                    g_wait_copy(way, hop, group).wait_recv()

                if hop + 1 < hops:

                    @pl.when(inside & sends(way, hop + 1))
                    def _():
                        g_copy(way, hop + 1, group).start()

    for group in range(groups):
        g_all[seq, group] = g_ref[:, group * LANES : (group + 1) * LANES]
    g_level(0)

    gain = gain_ref[...].astype(F32)
    aligned = piece_rows % 16 == 0

    def norm_piece(owner, piece, values):
        values = values.astype(F32)
        centred = values - jnp.mean(values, axis=-1, keepdims=True)
        spread = jnp.mean(centred * centred, axis=-1, keepdims=True)
        result = centred * lax.rsqrt(spread + 1e-05) * gain
        place = owner * pieces + piece
        if aligned:
            start = pl.multiple_of(place * piece_rows, 16)
            normed[pl.ds(start, piece_rows), :] = result.astype(BF16)
        else:
            normed32[place] = result

    for piece in range(pieces):
        norm_piece(tp, piece, x_ref[piece])
    for level in range(1, hops):
        g_level(level)
    for piece in range(pieces):
        for d in range(1, n_tp):
            x_copy(d, piece).wait_recv()
            norm_piece((tp + d) % n_tp, piece, x_all[d, piece])
    if not aligned:
        normed[...] = normed32[...].reshape(tokens, width).astype(BF16)

    w_copy.wait()
    for c in range(3):
        for group in range(groups):
            columns = slice(group * LANES, (group + 1) * LANES)
            proj[c, group] = mm(normed[...], w_ref[c, :, columns], 1, 0).astype(BF16)
    normed_t[...] = normed[...].T

    source = jnp.int32(0)
    live = jnp.int32(0)
    for rank in range(ids_ref.shape[1]):
        match = (ids_ref[0, rank] == seq) & (rank < count_ref[0])
        source = jnp.where(match, slot_ref[0, rank], source)
        live = jnp.where(match, 1, live)
    picks = [jnp.where(source == block, live, 0).astype(F32) for block in range(n_seq)]

    lane = lax.broadcasted_iota(jnp.int32, (1, LANES), 1)
    heads_here = LANES // HD
    masks = [
        ((lane >= h * HD) & (lane < (h + 1) * HD)).astype(F32).astype(BF16)
        for h in range(heads_here)
    ]

    def head(group, mask, cotangent):
        queries = proj[0, group]
        keys_own = proj[1, group] * mask
        values_own = proj[2, group] * mask
        scores = mm(keys_own, queries, 1, 1) * (HD**-0.5 * LOG2E)
        powers = jnp.exp2(scores - jnp.max(scores, axis=0, keepdims=True))
        attention = powers * (1.0 / jnp.sum(powers, axis=0, keepdims=True))
        grad_values = mm(attention.astype(BF16), cotangent * mask, 1, 0)
        grad_attention = mm(values_own, cotangent, 1, 1)
        weighted = attention * grad_attention
        inner = jnp.sum(weighted, axis=0, keepdims=True)
        scaled = ((weighted - attention * inner) * HD**-0.5).astype(BF16)
        grad_queries = mm(scaled, keys_own, 0, 0)
        grad_keys = mm(scaled, queries * mask, 1, 0)
        return grad_queries, grad_keys, grad_values

    def rows_of(who):
        return pl.ds(pl.multiple_of(who * block_rows, block_rows), block_rows)

    def copy1(group):
        return pltpu.make_async_remote_copy(
            src_ref=s1.at[group],
            dst_ref=r1.at[group],
            send_sem=s1_sem.at[group],
            recv_sem=r1_sem.at[group],
            device_id=at(g=y * n_core + other),
            device_id_type=MESH,
        )

    def copy2(group, d):
        return pltpu.make_async_remote_copy(
            src_ref=s2.at[group, d - 1],
            dst_ref=r2.at[group, d - 1],
            send_sem=s2_sem.at[group, d - 1],
            recv_sem=r2_sem.at[group, d - 1],
            device_id=at(g=((y + d) % n_y) * n_core + core),
            device_id_type=MESH,
        )

    def copy3(group, d):
        return pltpu.make_async_remote_copy(
            src_ref=s3.at[group, d - 1],
            dst_ref=r3.at[group, d - 1],
            send_sem=s3_sem.at[group, d - 1],
            recv_sem=r3_sem.at[group, d - 1],
            device_id=at(s=(seq + d) % n_seq),
            device_id_type=MESH,
        )

    def reduce1(group):
        if n_core > 1:
            for place in range(n_y):
                s1[group, place] = total[group, rows_of(place * n_core + other), :].astype(BF16)
            copy1(group).start()

    def reduce2(group):
        if n_core > 1:
            copy1(group).wait_recv()

        def part(place):
            mine = total[group, rows_of(place * n_core + core), :]
            return mine + r1[group, place].astype(F32) if n_core > 1 else mine

        for d in range(1, n_y):
            s2[group, d - 1] = part((y + d) % n_y).astype(BF16)
            copy2(group, d).start()
        acc[group] = part(y)

    def reduce3(group):
        for d in range(1, n_y):
            copy2(group, d).wait_recv()

        def part(place):
            rows = pl.ds(pl.multiple_of(place * out_rows, out_rows), out_rows)
            value = acc[group, rows, :]
            for d in range(1, n_y):
                value = value + r2[group, d - 1, rows, :].astype(F32)
            return value

        for d in range(1, n_seq):
            s3[group, d - 1] = part((seq + d) % n_seq).astype(BF16)
            copy3(group, d).start()
        acc[group, 0:out_rows, :] = part(seq)

    def reduce4(group):
        value = acc[group, 0:out_rows, :]
        for d in range(1, n_seq):
            copy3(group, d).wait_recv()
            value = value + r3[group, d - 1].astype(F32)
        return value

    def one_group(group, carry):
        g_level(hops + group)
        cotangent = g_all[0, group].astype(F32) * picks[0]
        for block in range(1, n_seq):
            cotangent = cotangent + g_all[block, group].astype(F32) * picks[block]
        cotangent = cotangent.astype(BF16)
        grads = head(group, masks[0], cotangent)

        @pl.when(group >= 1)
        def _():
            reduce2(group - 1)

        for mask in masks[1:]:
            more = head(group, mask, cotangent)
            grads = [a + b for a, b in zip(grads, more)]

        @pl.when(group >= 1)
        def _():
            reduce3(group - 1)

        joined = jnp.concatenate([grad.astype(BF16) for grad in grads], axis=1)
        product = mm(normed_t[...], joined, 1, 0)
        for c in range(3):
            total[group, c * width : (c + 1) * width, :] = product[:, c * LANES : (c + 1) * LANES]
        reduce1(group)
        return carry

    lax.fori_loop(0, groups, one_group, jnp.int32(0))
    reduce2(groups - 1)
    reduce3(groups - 1)
    for group in range(groups):
        out_ref[:, group * LANES : (group + 1) * LANES] = reduce4(group)

    for piece in range(pieces):
        for d in range(1, n_tp):
            x_copy(d, piece).wait_send()
    for hop in range(hops):
        for way in range(2):

            @pl.when(sends(way, hop))
            def _():
                for group in range(groups):
                    g_copy(way, hop, group).wait_send()

    for group in range(groups):
        if n_core > 1:
            copy1(group).wait_send()
        for d in range(1, n_y):
            copy2(group, d).wait_send()
        for d in range(1, n_seq):
            copy3(group, d).wait_send()


def body(sizes, crops, dout, crop_count, crop_ids, seq_slot, norm_gain, qkv_weight):
    n_grp, n_tp, n_seq, n_core = sizes
    n_y = n_grp // n_core
    tok_local, width = crops.shape[2], crops.shape[3]
    tokens, cols = dout.shape[2], dout.shape[3]
    groups = cols // LANES
    out_rows = 3 * width // (n_grp * n_seq)
    block_rows = n_seq * out_rows
    pieces = 3 if tok_local % 48 == 0 else 1
    piece_rows = tok_local // pieces
    aligned = piece_rows % 16 == 0
    hops = n_seq - 1
    vmem = pl.BlockSpec(memory_space=pltpu.VMEM)
    smem = pl.BlockSpec(memory_space=pltpu.SMEM)
    dma = pltpu.SemaphoreType.DMA
    scratch = [
        pltpu.VMEM((3, width, cols), BF16),
        pltpu.VMEM((n_tp, pieces, piece_rows, width), BF16),
        pltpu.VMEM((8, LANES) if aligned else (n_tp * pieces, piece_rows, width), F32),
        pltpu.VMEM((tokens, width), BF16),
        pltpu.VMEM((width, tokens), BF16),
        pltpu.VMEM((3, groups, tokens, LANES), BF16),
        pltpu.VMEM((n_seq, groups, tokens, LANES), BF16),
        pltpu.VMEM((groups, 3 * width, LANES), F32),
        pltpu.VMEM((groups, block_rows, LANES), F32),
        pltpu.VMEM((groups, n_y, block_rows, LANES), BF16),
        pltpu.VMEM((groups, n_y, block_rows, LANES), BF16),
        pltpu.VMEM((groups, max(n_y - 1, 1), block_rows, LANES), BF16),
        pltpu.VMEM((groups, max(n_y - 1, 1), block_rows, LANES), BF16),
        pltpu.VMEM((groups, max(n_seq - 1, 1), out_rows, LANES), BF16),
        pltpu.VMEM((groups, max(n_seq - 1, 1), out_rows, LANES), BF16),
        dma,
        dma((max(n_tp - 1, 1), pieces)),
        dma((max(n_tp - 1, 1), pieces)),
        dma((2, hops, groups)),
        dma((2, hops, groups)),
        dma((groups,)),
        dma((groups,)),
        dma((groups, max(n_y - 1, 1))),
        dma((groups, max(n_y - 1, 1))),
        dma((groups, n_seq - 1)),
        dma((groups, n_seq - 1)),
    ]
    return pl.pallas_call(
        functools.partial(kernel, sizes),
        out_shape=jax.ShapeDtypeStruct((out_rows, cols), F32),
        in_specs=[vmem, vmem, smem, smem, smem, vmem, pl.BlockSpec(memory_space=pl.ANY)],
        out_specs=vmem,
        scratch_shapes=scratch,
        compiler_params=pltpu.CompilerParams(
            collective_id=0, has_side_effects=True, vmem_limit_bytes=56 * 2**20
        ),
        cost_estimate=pl.CostEstimate(
            flops=22 * tokens * width * cols, bytes_accessed=8 * width * cols, transcendentals=0
        ),
    )(
        crops.reshape(pieces, piece_rows, width),
        dout.reshape(tokens, cols),
        crop_count,
        crop_ids,
        seq_slot,
        norm_gain.reshape(1, width),
        qkv_weight,
    )


def solution(mesh):
    n_grp, n_tp, n_seq = mesh.shape["grp"], mesh.shape["tp"], mesh.shape["seq"]
    n_core = 2 if n_grp % 2 == 0 else 1
    in_specs = (
        P("grp", "seq", "tp", None),
        P("grp", "seq", None, "tp"),
        P("grp"),
        P("grp", None),
        P("grp", None),
        P(),
        P(None, None, "tp"),
    )
    out_specs = P(("grp", "seq"), "tp")
    return jax.shard_map(
        functools.partial(body, (n_grp, n_tp, n_seq, n_core)),
        mesh=mesh,
        in_specs=in_specs,
        out_specs=out_specs,
        check_vma=False,
    )
```

time: 280 us -> 79 us (0.28)
  waiting for transfers between devices: 159 us -> 0 us
  matrix products: 77.4 us -> 0 us
  Pallas kernels: 0 us -> 75.1 us
  local copies, waits for them, and re-layouts: 25.3 us -> 3.05 us
  between operations: 14 us -> 0.66 us
  other arithmetic: 3.26 us -> 0 us
    reduce_scatter x1 -> x0, waiting for transfers between devices: 85.4 us -> none  [body(): lax.psum_scatter(grad_rows, ('grp', 'seq'), scatter_dimension=0, tiled=True)]
    pallas_call x0 -> x1, Pallas kernels: none -> 75.1 us  [body(): pl.pallas_call(functools.partial(kernel, sizes), out_shape=jax.ShapeDtype...]
    all_gather x2 -> x0, waiting for transfers between devices: 73.3 us -> none  [the longest x1 54 us: body(): lax.all_gather(crops, 'seq', axis=1, tiled=True)[0]]
    dot_general x7 -> x0, matrix products: 68.2 us -> none  [the longest x1 19.1 us: crop_grads(): jnp.einsum('ehqk,ekhd->eqhd', scaled, key_rows, preferred_element_type=jn...]
    sub x1 -> x0, matrix products: 9.23 us -> none  [crop_grads(): attention = jax.nn.softmax(scores, axis=-1)]
    slice x4 -> x0, local copies, waits for them, and re-layouts: 7.8 us -> none  [the longest x2 3.46 us: crop_grads(): value_rows = heads_view[2]]
    transpose x1 -> x0, local copies, waits for them, and re-layouts: 6.61 us -> none  [crop_grads(): jnp.einsum('etd,cetw->cdw', normed, stacked, preferred_element_type=jnp.f...]
    another operation x3 -> x0, local copies, waits for them, and re-layouts: 6.44 us -> none  [crop_grads(): jnp.stack([grad_queries, grad_keys, grad_values])]
  transfers between devices with their start and end apart: 3 -> 0, of which waited for: 3 -> 0; matrix products, arithmetic and copies ran while one was open for 1% -> 0% of each run, Pallas kernels for 0% -> 0%
where the time goes in v1:
time: 79 us; the launch traced here: 78.8 us
  Pallas kernels  75.1 us (95%)
  local copies, waits for them, and re-layouts  3.05 us (4%)
    pallas_call x1, Pallas kernels, body(): pl.pallas_call(functools.partial(kernel, sizes), out_shape=jax.ShapeDtype...  75.1 us
    unnamed x1, local copies, waits for them, and re-layouts  1.77 us

profile of v1, /device:TPU:0, one launch (start us, length us, event | category | flops | bytes accessed | tf_op | source)
XLA Modules:
  0.0 78.8 jit_solution(3028793523100198608)
XLA Ops:
  0.7 1.3 %reshape.11.gain_ref = bf16[1,1024]{1,0:T(2,128)(2,1)} reshape(bf16[1024]{0:T(1024)(128)(2,1)} %param.12) | data formatting | bytes 4096 | tf_op jit(solution)/shard_map/reshape | solution.py:416
  1.9 75.1 %shard_map.73 = f32[192,512]{1,0:T(8,128)} custom-call(bf16[3,96,1024]{2,1,0:T(8,128)(2,1)} %bitcast.2, bf16[576,512]{1,0:T(8,128)(2,1)} %bitcast.3, s32[1]{0:T(128)S(6)} %copy.9.count_ref, s32[1,4]{1,0:T(1,128)} %ids_ref.1, s32[1,4]{1,0:T(1,128)} %slot_ref.1, bf16[1,1024]{1,0:T(2,128)(2,1)} %reshape.11.gain_ref, bf16[3,1024,512]{2,1,0:T(8,128)(2,1)} %w_hbm.1), custom_call_target="tpu_custom_call" | custom-call | flops 6643777536 | bytes 4194304 | tf_op jit(solution)/shard_map/pallas_call | solution.py:398
  77.0 1.8 %copy.10 = f32[192,512]{1,0:T(8,128)} copy(f32[192,512]{1,0:T(8,128)} %shard_map.73) | data formatting | bytes 786432

commit v2 on v1

--- a/solution.py
+++ b/solution.py
@@ -36,6 +36,7 @@
     normed_t,
     proj,
     g_all,
+    picked,
     total,
     acc,
     s1,
@@ -126,13 +127,53 @@
             device_id_type=MESH,
         )
 
+    def position(way):
+        return seq if way == 0 else n_seq - 1 - seq
+
     def sends(way, hop):
-        if way == 0:
-            return (seq >= hop) & (seq + 1 < n_seq)
-        return (seq + hop < n_seq) & (seq >= 1)
+        where = position(way)
+        if hop == hops - 1:
+            return where == n_seq - 2
+        return (where >= hop) & (where <= n_seq - 3)
 
     def receives(way, hop):
-        return seq >= hop + 1 if way == 0 else seq + hop + 1 < n_seq
+        where = position(way)
+        if hop == hops - 1:
+            return where == n_seq - 1
+        return (where >= hop + 1) & (where <= n_seq - 2)
+
+    def picks_of(who):
+        source = jnp.int32(0)
+        live = jnp.int32(0)
+        for rank in range(ids_ref.shape[1]):
+            match = (ids_ref[0, rank] == who) & (rank < count_ref[0])
+            source = jnp.where(match, slot_ref[0, rank], source)
+            live = jnp.where(match, 1, live)
+        return [jnp.where(source == block, live, 0).astype(F32) for block in range(n_seq)]
+
+    end_picks = [picks_of(n_seq - 1), picks_of(0)]
+
+    def pick_copy(way, group):
+        step = 1 if way == 0 else -1
+        return pltpu.make_async_remote_copy(
+            src_ref=picked.at[way, group],
+            dst_ref=g_all.at[seq, group],
+            send_sem=gs_sem.at[way, hops - 1, group],
+            recv_sem=gr_sem.at[way, hops - 1, group],
+            device_id=at(s=seq + step),
+            device_id_type=MESH,
+        )
+
+    def pick_wait_copy(way, group):
+        step = 1 if way == 0 else -1
+        return pltpu.make_async_remote_copy(
+            src_ref=picked.at[way, group],
+            dst_ref=g_all.at[seq - step, group],
+            send_sem=gs_sem.at[way, hops - 1, group],
+            recv_sem=gr_sem.at[way, hops - 1, group],
+            device_id=at(s=seq - step),
+            device_id_type=MESH,
+        )
 
     def g_level(level):
         for way in range(2):
@@ -148,16 +189,37 @@
 
                 @pl.when(inside & receives(way, hop))
                 def _():
-                    g_wait_copy(way, hop, group).wait_recv()
-
-                if hop + 1 < hops:
+                    if hop == hops - 1:
+                        pick_wait_copy(way, group).wait_recv()
+                    else:
+                        g_wait_copy(way, hop, group).wait_recv()
+
+                if hop + 1 < hops - 1:
 
                     @pl.when(inside & sends(way, hop + 1))
                     def _():
                         g_copy(way, hop + 1, group).start()
 
+                if hop + 1 == hops - 1:
+
+                    @pl.when(inside & sends(way, hop + 1))
+                    def _():
+                        blocks = range(n_seq - 1) if way == 0 else range(1, n_seq)
+                        value = jnp.zeros((tokens, LANES), F32)
+                        for block in blocks:
+                            value = value + g_all[block, group].astype(F32) * end_picks[way][block]
+                        picked[way, group] = value.astype(BF16)
+                        pick_copy(way, group).start()
+
     for group in range(groups):
         g_all[seq, group] = g_ref[:, group * LANES : (group + 1) * LANES]
+    for way in range(2):
+
+        @pl.when(position(way) == n_seq - 1)
+        def _():
+            for block in range(n_seq - 2) if way == 0 else range(2, n_seq):
+                g_all[block] = jnp.zeros(g_all.shape[1:], BF16)
+
     g_level(0)
 
     gain = gain_ref[...].astype(F32)
@@ -179,27 +241,37 @@
         norm_piece(tp, piece, x_ref[piece])
     for level in range(1, hops):
         g_level(level)
+    w_copy.wait()
+
+    def project(owner):
+        rows = pl.ds(pl.multiple_of(owner * pieces * piece_rows, 16), pieces * piece_rows)
+        for c in range(3):
+            for group in range(groups):
+                columns = slice(group * LANES, (group + 1) * LANES)
+                result = mm(normed[rows, :], w_ref[c, :, columns], 1, 0)
+                proj[c, group, rows, :] = result.astype(BF16)
+
+    if aligned:
+        project(tp)
     for piece in range(pieces):
         for d in range(1, n_tp):
             x_copy(d, piece).wait_recv()
             norm_piece((tp + d) % n_tp, piece, x_all[d, piece])
-    if not aligned:
+    if aligned:
+        for d in range(1, n_tp):
+            project((tp + d) % n_tp)
+    else:
         normed[...] = normed32[...].reshape(tokens, width).astype(BF16)
-
-    w_copy.wait()
-    for c in range(3):
-        for group in range(groups):
-            columns = slice(group * LANES, (group + 1) * LANES)
-            proj[c, group] = mm(normed[...], w_ref[c, :, columns], 1, 0).astype(BF16)
+        for c in range(3):
+            for group in range(groups):
+                columns = slice(group * LANES, (group + 1) * LANES)
+                proj[c, group] = mm(normed[...], w_ref[c, :, columns], 1, 0).astype(BF16)
     normed_t[...] = normed[...].T
 
-    source = jnp.int32(0)
-    live = jnp.int32(0)
-    for rank in range(ids_ref.shape[1]):
-        match = (ids_ref[0, rank] == seq) & (rank < count_ref[0])
-        source = jnp.where(match, slot_ref[0, rank], source)
-        live = jnp.where(match, 1, live)
-    picks = [jnp.where(source == block, live, 0).astype(F32) for block in range(n_seq)]
+    picks = picks_of(seq)
+    for block in range(n_seq):
+        sent = ((seq == n_seq - 1) & (block == n_seq - 2)) | ((seq == 0) & (block == 1))
+        picks[block] = jnp.where(sent, 1.0, picks[block])
 
     lane = lax.broadcasted_iota(jnp.int32, (1, LANES), 1)
     heads_here = LANES // HD
@@ -311,13 +383,13 @@
         def _():
             reduce2(group - 1)
 
+        @pl.when(group >= 2)
+        def _():
+            reduce3(group - 2)
+
         for mask in masks[1:]:
             more = head(group, mask, cotangent)
             grads = [a + b for a, b in zip(grads, more)]
-
-        @pl.when(group >= 1)
-        def _():
-            reduce3(group - 1)
 
         joined = jnp.concatenate([grad.astype(BF16) for grad in grads], axis=1)
         product = mm(normed_t[...], joined, 1, 0)
@@ -328,7 +400,8 @@
 
     lax.fori_loop(0, groups, one_group, jnp.int32(0))
     reduce2(groups - 1)
-    reduce3(groups - 1)
+    for group in range(max(groups - 2, 0), groups):
+        reduce3(group)
     for group in range(groups):
         out_ref[:, group * LANES : (group + 1) * LANES] = reduce4(group)
 
@@ -341,7 +414,8 @@
             @pl.when(sends(way, hop))
             def _():
                 for group in range(groups):
-                    g_copy(way, hop, group).wait_send()
+                    copy = pick_copy(way, group) if hop == hops - 1 else g_copy(way, hop, group)
+                    copy.wait_send()
 
     for group in range(groups):
         if n_core > 1:
@@ -375,6 +449,7 @@
         pltpu.VMEM((width, tokens), BF16),
         pltpu.VMEM((3, groups, tokens, LANES), BF16),
         pltpu.VMEM((n_seq, groups, tokens, LANES), BF16),
+        pltpu.VMEM((2, groups, tokens, LANES), BF16),
         pltpu.VMEM((groups, 3 * width, LANES), F32),
         pltpu.VMEM((groups, block_rows, LANES), F32),
         pltpu.VMEM((groups, n_y, block_rows, LANES), BF16),

time: 79 us -> 64 us (0.81)
  Pallas kernels: 75.1 us -> 60.1 us
    pallas_call x1, Pallas kernels: 75.1 us -> 60.1 us  [body(): pl.pallas_call(functools.partial(kernel, sizes), out_shape=jax.ShapeDtype...]
where the time goes in v2:
time: 64 us; the launch traced here: 63.8 us
  Pallas kernels  60.1 us (94%)
  local copies, waits for them, and re-layouts  3.05 us (5%)
  between operations  0.66 us (1%)
    pallas_call x1, Pallas kernels, body(): pl.pallas_call(functools.partial(kernel, sizes), out_shape=jax.ShapeDtype...  60.1 us
    unnamed x1, local copies, waits for them, and re-layouts  1.77 us

profile of v2, /device:TPU:0, one launch (start us, length us, event | category | flops | bytes accessed | tf_op | source)
XLA Modules:
  0.0 63.8 jit_solution(14244972258380764840)
XLA Ops:
  0.7 1.3 %reshape.11.gain_ref = bf16[1,1024]{1,0:T(2,128)(2,1)} reshape(bf16[1024]{0:T(1024)(128)(2,1)} %param.12) | data formatting | bytes 4096 | tf_op jit(solution)/shard_map/reshape | solution.py:491
  1.9 60.1 %shard_map.73 = f32[192,512]{1,0:T(8,128)} custom-call(bf16[3,96,1024]{2,1,0:T(8,128)(2,1)} %bitcast.2, bf16[576,512]{1,0:T(8,128)(2,1)} %bitcast.3, s32[1]{0:T(128)S(6)} %copy.9.count_ref, s32[1,4]{1,0:T(1,128)} %ids_ref.1, s32[1,4]{1,0:T(1,128)} %slot_ref.1, bf16[1,1024]{1,0:T(2,128)(2,1)} %reshape.11.gain_ref, bf16[3,1024,512]{2,1,0:T(8,128)(2,1)} %w_hbm.1), custom_call_target="tpu_custom_call" | custom-call | flops 6643777536 | bytes 4194304 | tf_op jit(solution)/shard_map/pallas_call | solution.py:473
  62.0 1.8 %copy.10 = f32[192,512]{1,0:T(8,128)} copy(f32[192,512]{1,0:T(8,128)} %shard_map.73) | data formatting | bytes 786432

commit v3 on v2

--- a/solution.py
+++ b/solution.py
@@ -39,6 +39,7 @@
     picked,
     total,
     acc,
+    own,
     s1,
     r1,
     s2,
@@ -309,12 +310,16 @@
             device_id_type=MESH,
         )
 
-    def copy2(group, d):
-        return pltpu.make_async_remote_copy(
-            src_ref=s2.at[group, d - 1],
-            dst_ref=r2.at[group, d - 1],
-            send_sem=s2_sem.at[group, d - 1],
-            recv_sem=r2_sem.at[group, d - 1],
+    def owner_rows(e):
+        place = (seq + e) % n_seq
+        return pl.ds(pl.multiple_of(place * out_rows, out_rows), out_rows)
+
+    def copy2(group, d, e):
+        return pltpu.make_async_remote_copy(
+            src_ref=s2.at[group, d - 1, owner_rows(e)],
+            dst_ref=r2.at[group, d - 1, owner_rows(e)],
+            send_sem=s2_sem.at[group, d - 1, e],
+            recv_sem=r2_sem.at[group, d - 1, e],
             device_id=at(g=((y + d) % n_y) * n_core + core),
             device_id_type=MESH,
         )
@@ -343,29 +348,28 @@
             mine = total[group, rows_of(place * n_core + core), :]
             return mine + r1[group, place].astype(F32) if n_core > 1 else mine
 
+        order = list(range(1, n_seq)) + [0]
         for d in range(1, n_y):
             s2[group, d - 1] = part((y + d) % n_y).astype(BF16)
-            copy2(group, d).start()
+            for e in order:
+                copy2(group, d, e).start()
         acc[group] = part(y)
 
     def reduce3(group):
-        for d in range(1, n_y):
-            copy2(group, d).wait_recv()
-
-        def part(place):
-            rows = pl.ds(pl.multiple_of(place * out_rows, out_rows), out_rows)
-            value = acc[group, rows, :]
+        def part(e):
+            value = acc[group, owner_rows(e), :]
             for d in range(1, n_y):
-                value = value + r2[group, d - 1, rows, :].astype(F32)
+                copy2(group, d, e).wait_recv()
+                value = value + r2[group, d - 1, owner_rows(e), :].astype(F32)
             return value
 
-        for d in range(1, n_seq):
-            s3[group, d - 1] = part((seq + d) % n_seq).astype(BF16)
-            copy3(group, d).start()
-        acc[group, 0:out_rows, :] = part(seq)
+        for e in range(1, n_seq):
+            s3[group, e - 1] = part(e).astype(BF16)
+            copy3(group, e).start()
+        own[group] = part(0)
 
     def reduce4(group):
-        value = acc[group, 0:out_rows, :]
+        value = own[group]
         for d in range(1, n_seq):
             copy3(group, d).wait_recv()
             value = value + r3[group, d - 1].astype(F32)
@@ -421,7 +425,8 @@
         if n_core > 1:
             copy1(group).wait_send()
         for d in range(1, n_y):
-            copy2(group, d).wait_send()
+            for e in range(n_seq):
+                copy2(group, d, e).wait_send()
         for d in range(1, n_seq):
             copy3(group, d).wait_send()
 
@@ -452,6 +457,7 @@
         pltpu.VMEM((2, groups, tokens, LANES), BF16),
         pltpu.VMEM((groups, 3 * width, LANES), F32),
         pltpu.VMEM((groups, block_rows, LANES), F32),
+        pltpu.VMEM((groups, out_rows, LANES), F32),
         pltpu.VMEM((groups, n_y, block_rows, LANES), BF16),
         pltpu.VMEM((groups, n_y, block_rows, LANES), BF16),
         pltpu.VMEM((groups, max(n_y - 1, 1), block_rows, LANES), BF16),
@@ -465,8 +471,8 @@
         dma((2, hops, groups)),
         dma((groups,)),
         dma((groups,)),
-        dma((groups, max(n_y - 1, 1))),
-        dma((groups, max(n_y - 1, 1))),
+        dma((groups, max(n_y - 1, 1), n_seq)),
+        dma((groups, max(n_y - 1, 1), n_seq)),
         dma((groups, n_seq - 1)),
         dma((groups, n_seq - 1)),
     ]

time: 64 us -> 63.2 us (0.988)
  Pallas kernels: 60.1 us -> 59.3 us
    pallas_call x1, Pallas kernels: 60.1 us -> 59.3 us  [body(): pl.pallas_call(functools.partial(kernel, sizes), out_shape=jax.ShapeDtype...]
where the time goes in v3:
time: 63.2 us; the launch traced here: 63 us
  Pallas kernels  59.3 us (94%)
  local copies, waits for them, and re-layouts  3.05 us (5%)
  between operations  0.66 us (1%)
    pallas_call x1, Pallas kernels, body(): pl.pallas_call(functools.partial(kernel, sizes), out_shape=jax.ShapeDtype...  59.3 us
    unnamed x1, local copies, waits for them, and re-layouts  1.77 us
    reshape x1, local copies, waits for them, and re-layouts, body(): norm_gain.reshape(1, width)  1.28 us

profile of v3, /device:TPU:0, one launch (start us, length us, event | category | flops | bytes accessed | tf_op | source)
XLA Modules:
  0.0 63.0 jit_solution(6198812735113728878)
XLA Ops:
  0.7 1.3 %reshape.11.gain_ref = bf16[1,1024]{1,0:T(2,128)(2,1)} reshape(bf16[1024]{0:T(1024)(128)(2,1)} %param.12) | data formatting | bytes 4096 | tf_op jit(solution)/shard_map/reshape | solution.py:497
  1.9 59.3 %shard_map.73 = f32[192,512]{1,0:T(8,128)} custom-call(bf16[3,96,1024]{2,1,0:T(8,128)(2,1)} %bitcast.2, bf16[576,512]{1,0:T(8,128)(2,1)} %bitcast.3, s32[1]{0:T(128)S(6)} %copy.9.count_ref, s32[1,4]{1,0:T(1,128)} %ids_ref.1, s32[1,4]{1,0:T(1,128)} %slot_ref.1, bf16[1,1024]{1,0:T(2,128)(2,1)} %reshape.11.gain_ref, bf16[3,1024,512]{2,1,0:T(8,128)(2,1)} %w_hbm.1), custom_call_target="tpu_custom_call" | custom-call | flops 6643777536 | bytes 4194304 | tf_op jit(solution)/shard_map/pallas_call | solution.py:479
  61.2 1.8 %copy.10 = f32[192,512]{1,0:T(8,128)} copy(f32[192,512]{1,0:T(8,128)} %shard_map.73) | data formatting | bytes 786432
